TPU v7x, 512 devices: a whole 4x4x16 slice. The times are simulated.
512 devices in a mesh: section: 32 (over z, y_hi), tensor: 8 (over x, y_lo), dp: 2 (over core).
Axes of the slice: x: 4, y: 4 (y_hi: 2, y_lo: 2; y = y_hi * 2 + y_lo), z: 16, core: 2. Of those that a mesh axis runs over, the one named last changes fastest.
Arguments:
- start_acts: bfloat16 [32, 256, 5120], P('section', 'dp', 'tensor'), may hold values from -6 to 6
- fresh_acts: bfloat16 [2, 256, 5120], P(None, 'dp', 'tensor'), may hold values from -6 to 6
- ln_gain: float32 [32, 5120], P('section'), may hold values from 0.1 to 1.9
- ln_shift: float32 [32, 5120], P('section'), may hold values from -4 to 4
- proj: bfloat16 [32, 5120, 5120], P('section', 'dp', 'tensor'), may hold values from -0.078125 to 0.078125
- proj_bias: float32 [32, 5120], P('section', 'tensor'), may hold values from -6 to 6
- sample_ids: int32 [34, 4], P(None, 'dp'), may hold values from 0 to 3
- base_out: bfloat16 [32, 8, 64, 5120], P('section', 'dp', None, 'tensor'), may hold values from -6 to 6
- base_in: bfloat16 [32, 8, 64, 5120], P('section', 'dp', None, 'tensor'), may hold values from -6 to 6
- scale_exps: int32 [32, 3, 256, 40], P('section', None, 'dp', 'tensor'), may hold values from -1 to 2
Outputs:
- layer_out: bfloat16 [32, 3, 256, 5120], P('section', None, 'dp', 'tensor')
- last_arrived: bfloat16 [32, 256, 5120], P('section', 'dp', 'tensor')
Inputs may be any that keep to these rules, and one draw needn't show every extreme that they name: `sample_ids`: each replica stores 4 samples; an id names a slot within its own replica's store.
All inputs are finite; a program needn't handle non-finite values.
Results may differ from a plain program's by a relative error of at most 0.012.
Values may be sent and summed in bfloat16 or wider, within the bound.
No kernel may reach another device: no remote copies, remote signals or barrier semaphores. Data moves between devices by JAX's collectives and lax.ppermute only.
A program may use at most 64 MiB of HBM per device.

v0:
```python
import jax
import jax.numpy as jnp
from jax import lax
from jax.sharding import PartitionSpec as P

TICKS = 3


norm_eps = 1e-05
clip_limit = 4.0


def from_behind(value, axis, steps):
    count = lax.axis_size(axis)
    first, last = (max(0, -steps), min(count, count - steps))
    return lax.ppermute(value, axis, [(source, source + steps) for source in range(first, last)])


def normalize(values, gain_row, shift_row):
    average = jnp.mean(values, axis=-1, keepdims=True)
    centered = values - average
    spread = jnp.mean(centered * centered, axis=-1, keepdims=True)
    return (centered * lax.rsqrt(spread + norm_eps) * gain_row + shift_row).astype(jnp.bfloat16)


def block_factor(factors, block_width):
    return jnp.repeat(factors.astype(jnp.float32), block_width, axis=-1)


def shards(
    start_acts,
    fresh_acts,
    ln_gain,
    ln_shift,
    proj,
    proj_bias,
    sample_ids,
    base_out,
    base_in,
    scale_exps,
):
    section_id = lax.axis_index("section")
    sections = lax.axis_size("section")
    micro = sample_ids.shape[0]
    row_count = start_acts.shape[1]
    col_count = start_acts.shape[2]
    block_width = col_count // scale_exps.shape[3]
    weight_local = proj[0]

    def lookup(base_table, batch_index):
        ids_row = lax.dynamic_index_in_dim(sample_ids, batch_index, 0, keepdims=False)
        picked = jnp.take(base_table[0], ids_row, axis=0)
        return picked.reshape(row_count, col_count).astype(jnp.float32)

    weight_all = lax.all_gather(weight_local, "dp", axis=0, tiled=True)
    current = start_acts[0]
    outputs = []
    arrived = current
    for step_no in range(TICKS):
        full_rows = lax.all_gather(current, "tensor", axis=1, tiled=True)
        normed = normalize(full_rows.astype(jnp.float32), ln_gain[0], ln_shift[0])
        projected = jnp.dot(normed, weight_all, preferred_element_type=jnp.float32)
        result = (current.astype(jnp.float32) + jax.nn.relu(projected + proj_bias[0])).astype(
            jnp.bfloat16
        )
        outputs.append(result)
        batch_index = step_no + sections - 1 - section_id
        factors = jnp.exp2(scale_exps[0, step_no].astype(jnp.float32))
        delta = result.astype(jnp.float32) - lookup(base_out, batch_index)
        coded = jnp.clip(
            delta / block_factor(factors, block_width), -clip_limit, clip_limit
        ).astype(jnp.bfloat16)
        coded_in, factor_in = from_behind((coded, factors.astype(jnp.bfloat16)), "section", 1)
        recv_index = jnp.minimum(batch_index + 1, micro - 1)
        rebuilt = lookup(base_in, recv_index) + coded_in.astype(jnp.float32) * block_factor(
            factor_in, block_width
        )
        arrived = jnp.where(section_id > 0, rebuilt, jnp.zeros_like(rebuilt)).astype(jnp.bfloat16)
        if step_no + 1 < TICKS:
            current = jnp.where(section_id > 0, arrived, fresh_acts[step_no])
    return (jnp.stack(outputs, axis=0)[None], arrived[None])


def solution(mesh):
    return jax.shard_map(
        shards,
        mesh=mesh,
        in_specs=(
            P("section", "dp", "tensor"),
            P(None, "dp", "tensor"),
            P("section", None),
            P("section", None),
            P("section", "dp", "tensor"),
            P("section", "tensor"),
            P(None, "dp"),
            P("section", "dp", None, "tensor"),
            P("section", "dp", None, "tensor"),
            P("section", None, "dp", "tensor"),
        ),
        out_specs=(P("section", None, "dp", "tensor"), P("section", "dp", "tensor")),
        check_vma=False,
    )
```

profile of v0, /device:TPU:136, one launch (start us, length us, event | category | flops | bytes accessed | tf_op | source)
XLA Modules:
  0.0 252.5 jit_solution(7556862004391863116)
XLA Ops:
  8.8 4.2 %collective-permute-start.1 = (bf16[128,5]{0,1:T(8,128)(2,1)S(1)}, bf16[128,5]{0,1:T(8,128)(2,1)S(1)}, u32[]{:S(2)}, u32[]{:S(2)}) collective-permute-start(bf16[128,5]{0,1:T(8,128)(2,1)S(1)} %bitcast.138), channel_id=1, source_target_pairs={{0,16},{16,32},{32,48},{48,64},{64,80},{80,96},{96,112},{112,128},... | collective-permute-start | bytes 3848 | tf_op jit(solution)/shard_map/ppermute | solution.py:16
  14.9 47.6 %all-gather.11.cloned.1.call-done = bf16[1,128,5120]{2,1,0:T(8,128)(2,1)} async-done(((bf16[1,128,640]{2,1,0:T(8,128)(2,1)}), bf16[1,128,5120]{2,1,0:T(8,128)(2,1)}) %all-gather.11.cloned.1.call-update) | async-done | bytes 1310736 | tf_op jit(solution)/shard_map/all_gather | solution.py:60
  62.5 1.7 convert_reduce_fusion
  64.2 1.8 fusion.21
  66.0 26.8 %all-gather.13.cloned.1.call-done = bf16[1,5120,640]{2,1,0:T(8,128)(2,1)} async-done(((bf16[1,2560,640]{2,1,0:T(8,128)(2,1)}), bf16[1,5120,640]{2,1,0:T(8,128)(2,1)}) %all-gather.13.cloned.1.call-update) | async-done | bytes 6553616 | tf_op jit(solution)/shard_map/all_gather | solution.py:55
  92.8 4.2 %fusion.112 = (bf16[128,640]{1,0:T(8,128)(2,1)S(1)}, bf16[128,640]{1,0:T(8,128)(2,1)S(1)}) fusion(f32[128,640]{1,0:T(8,128)S(1)} %copy.18, bf16[2,64,640]{2,1,0:T(8,128)(2,1)S(1)} %broadcast_select_fusion.4, f32[640]{0:T(1024)S(1)} %reduce.1, bf16[1,5120,640]{2,1,0:T(8,128)(2,1)} %all-gather.13.cloned.1.call-done, bf16[1,128,5120]{2,1,0:T(8,128)(2,1)S(1)} %copy-done.1, ...), kind=kOutput, calls=%fused_computation.79 | convolution fusion | flops 843694080 | bytes 8891904 | tf_op jit(solution)/shard_map/dot_general | solution.py:62
  97.1 4.0 %collective-permute-start = (bf16[128,640]{1,0:T(8,128)(2,1)S(1)}, bf16[128,640]{1,0:T(8,128)(2,1)S(1)}, u32[]{:S(2)}, u32[]{:S(2)}) collective-permute-start(bf16[128,640]{1,0:T(8,128)(2,1)S(1)} %get-tuple-element.12), channel_id=1, source_target_pairs={{0,16},{16,32},{32,48},{48,64},{64,80},{80,96},{96,112},{112,128},... | collective-permute-start | bytes 491528 | tf_op jit(solution)/shard_map/ppermute | solution.py:16
  101.4 7.6 %collective-permute-done = bf16[128,640]{1,0:T(8,128)(2,1)S(1)} collective-permute-done((bf16[128,640]{1,0:T(8,128)(2,1)S(1)}, bf16[128,640]{1,0:T(8,128)(2,1)S(1)}, u32[]{:S(2)}, u32[]{:S(2)}) %collective-permute-start) | collective-permute-done | bytes 163872 | tf_op jit(solution)/shard_map/ppermute | solution.py:16
  109.0 0.8 fusion.115
  109.9 1.9 collective-permute-start.3
  113.3 45.8 %all-gather.7.cloned.1.call-done = bf16[128,5120]{1,0:T(8,128)(2,1)} async-done(((bf16[128,640]{1,0:T(8,128)(2,1)}), bf16[128,5120]{1,0:T(8,128)(2,1)}) %all-gather.7.cloned.1.call-update) | async-done | bytes 1310736 | tf_op jit(solution)/shard_map/all_gather | solution.py:60
  159.1 1.7 convert_reduce_fusion.2
  160.8 1.8 fusion.14
  162.7 4.2 %fusion.107 = (bf16[128,640]{1,0:T(8,128)(2,1)S(1)}, bf16[128,640]{1,0:T(8,128)(2,1)S(1)}) fusion(f32[128,640]{1,0:T(8,128)S(1)} %copy.20, bf16[2,64,640]{2,1,0:T(8,128)(2,1)S(1)} %broadcast_select_fusion.2, f32[640]{0:T(1024)S(1)} %reduce.1, bf16[1,5120,640]{2,1,0:T(8,128)(2,1)} %all-gather.13.cloned.1.call-done, bf16[128,5120]{1,0:T(8,128)(2,1)S(1)} %copy-done.2, ...), kind=kOutput, calls=%fused_computation.72 | convolution fusion | flops 843694080 | bytes 8891904 | tf_op jit(solution)/shard_map/dot_general | solution.py:62
  166.9 4.5 %collective-permute-start.2 = (bf16[128,640]{1,0:T(8,128)(2,1)S(1)}, bf16[128,640]{1,0:T(8,128)(2,1)S(1)}, u32[]{:S(2)}, u32[]{:S(2)}) collective-permute-start(bf16[128,640]{1,0:T(8,128)(2,1)S(1)} %get-tuple-element.14), channel_id=1, source_target_pairs={{0,16},{16,32},{32,48},{48,64},{64,80},{80,96},{96,112},{112,128},... | collective-permute-start | bytes 491528 | tf_op jit(solution)/shard_map/ppermute | solution.py:16
  171.7 6.0 %collective-permute-done.2 = bf16[128,640]{1,0:T(8,128)(2,1)S(1)} collective-permute-done((bf16[128,640]{1,0:T(8,128)(2,1)S(1)}, bf16[128,640]{1,0:T(8,128)(2,1)S(1)}, u32[]{:S(2)}, u32[]{:S(2)}) %collective-permute-start.2) | collective-permute-done | bytes 163872 | tf_op jit(solution)/shard_map/ppermute | solution.py:16
  178.5 2.5 collective-permute-start.5
  182.6 44.1 %all-gather.9.cloned.1.call-done = bf16[128,5120]{1,0:T(8,128)(2,1)} async-done(((bf16[128,640]{1,0:T(8,128)(2,1)}), bf16[128,5120]{1,0:T(8,128)(2,1)}) %all-gather.9.cloned.1.call-update) | async-done | bytes 1310736 | tf_op jit(solution)/shard_map/all_gather | solution.py:60
  226.7 1.7 convert_reduce_fusion.1
  228.4 1.8 fusion.10
  230.2 4.2 %fusion.102 = (bf16[128,640]{1,0:T(8,128)(2,1)S(1)}, bf16[128,640]{1,0:T(8,128)(2,1)S(1)}) fusion(f32[128,640]{1,0:T(8,128)S(1)} %copy.22, bf16[2,64,640]{2,1,0:T(8,128)(2,1)S(1)} %broadcast_select_fusion, f32[640]{0:T(1024)S(1)} %reduce.1, bf16[1,5120,640]{2,1,0:T(8,128)(2,1)} %all-gather.13.cloned.1.call-done, bf16[128,5120]{1,0:T(8,128)(2,1)S(1)} %copy-done.3, ...), kind=kOutput, calls=%fused_computation.65 | convolution fusion | flops 843694080 | bytes 8891904 | tf_op jit(solution)/shard_map/dot_general | solution.py:62
  234.4 4.5 %collective-permute-start.4 = (bf16[128,640]{1,0:T(8,128)(2,1)S(1)}, bf16[128,640]{1,0:T(8,128)(2,1)S(1)}, u32[]{:S(2)}, u32[]{:S(2)}) collective-permute-start(bf16[128,640]{1,0:T(8,128)(2,1)S(1)} %get-tuple-element.16), channel_id=1, source_target_pairs={{0,16},{16,32},{32,48},{48,64},{64,80},{80,96},{96,112},{112,128},... | collective-permute-start | bytes 491528 | tf_op jit(solution)/shard_map/ppermute | solution.py:16
  239.2 0.9 maximum_bitcast_fusion
  240.0 5.2 %collective-permute-done.4 = bf16[128,640]{1,0:T(8,128)(2,1)S(1)} collective-permute-done((bf16[128,640]{1,0:T(8,128)(2,1)S(1)}, bf16[128,640]{1,0:T(8,128)(2,1)S(1)}, u32[]{:S(2)}, u32[]{:S(2)}) %collective-permute-start.4) | collective-permute-done | bytes 163872 | tf_op jit(solution)/shard_map/ppermute | solution.py:16
  (94 shorter events, 8.7 us)
Async XLA Ops:
  7.2 6.4 %copy-start = (bf16[1,4,64,640]{3,2,1,0:T(8,128)(2,1)S(1)}, bf16[1,4,64,640]{3,2,1,0:T(8,128)(2,1)}, u32[]{:S(2)}) copy-start(bf16[1,4,64,640]{3,2,1,0:T(8,128)(2,1)} %param.19) | copy-start | bytes 983044
  7.2 1.6 copy-start.10
  7.2 6.1 %copy-start.9 = (s32[34,2]{0,1:T(2,128)S(1)}, s32[34,2]{0,1:T(2,128)}, u32[]{:S(2)}) copy-start(s32[34,2]{0,1:T(2,128)} %param.18) | copy-start | bytes 820
  7.2 7.0 %copy-start.11 = (f32[1,640]{1,0:T(1,128)S(1)}, f32[1,640]{1,0:T(1,128)}, u32[]{:S(2)}) copy-start(f32[1,640]{1,0:T(1,128)} %param.17) | copy-start | bytes 7684
  7.2 7.0 %copy-start.4 = (bf16[1,4,64,640]{3,2,1,0:T(8,128)(2,1)S(1)}, bf16[1,4,64,640]{3,2,1,0:T(8,128)(2,1)}, u32[]{:S(2)}) copy-start(bf16[1,4,64,640]{3,2,1,0:T(8,128)(2,1)} %param.20) | copy-start | bytes 983044
  7.2 55.3 %all-gather.11.cloned.1.call-start = ((), (), s32[]{:S(2)}) async-start(), calls=%async_computation.2 | async-start | bytes 1474560 | tf_op jit(solution)/shard_map/all_gather | solution.py:60
  8.0 84.9 %all-gather.13.cloned.1.call-start = ((), (), s32[]{:S(2)}) async-start(), calls=%async_computation.3 | async-start | bytes 9830400 | tf_op jit(solution)/shard_map/all_gather | solution.py:55
  8.7 84.1 %copy-start.8 = (bf16[1,128,640]{2,1,0:T(8,128)(2,1)S(1)}, bf16[1,128,640]{2,1,0:T(8,128)(2,1)}, u32[]{:S(2)}) copy-start(bf16[1,128,640]{2,1,0:T(8,128)(2,1)} %param.12) | copy-start | bytes 491524
  8.7 84.1 %copy-start.12 = (f32[1,5120]{1,0:T(1,128)S(1)}, f32[1,5120]{1,0:T(1,128)}, u32[]{:S(2)}) copy-start(f32[1,5120]{1,0:T(1,128)} %param.15) | copy-start | bytes 61444
  8.7 84.1 %copy-start.13 = (f32[1,5120]{1,0:T(1,128)S(1)}, f32[1,5120]{1,0:T(1,128)}, u32[]{:S(2)}) copy-start(f32[1,5120]{1,0:T(1,128)} %param.14) | copy-start | bytes 61444
  8.7 150.4 %all-gather.7.cloned.1.call-start = ((), (), s32[]{:S(2)}) async-start(), calls=%async_computation | async-start | bytes 1474560 | tf_op jit(solution)/shard_map/all_gather | solution.py:60
  8.8 92.4 %collective-permute-start.1 = (bf16[128,5]{0,1:T(8,128)(2,1)S(1)}, bf16[128,5]{0,1:T(8,128)(2,1)S(1)}, u32[]{:S(2)}, u32[]{:S(2)}) collective-permute-start(bf16[128,5]{0,1:T(8,128)(2,1)S(1)} %bitcast.138), channel_id=1, source_target_pairs={{0,16},{16,32},{32,48},{48,64},{64,80},{80,96},{96,112},{112,128},... | collective-permute-start | bytes 3848 | tf_op jit(solution)/shard_map/ppermute | solution.py:16
  62.5 30.3 %copy-start.1 = (bf16[1,128,5120]{2,1,0:T(8,128)(2,1)S(1)}, bf16[1,128,5120]{2,1,0:T(8,128)(2,1)}, u32[]{:S(2)}) copy-start(bf16[1,128,5120]{2,1,0:T(8,128)(2,1)} %all-gather.11.cloned.1.call-done) | copy-start | bytes 3932164
  92.8 16.2 %copy-start.7 = (bf16[2,128,640]{2,1,0:T(8,128)(2,1)S(1)}, bf16[2,128,640]{2,1,0:T(8,128)(2,1)}, u32[]{:S(2)}) copy-start(bf16[2,128,640]{2,1,0:T(8,128)(2,1)} %param.13) | copy-start | bytes 983044
  97.1 11.9 %collective-permute-start = (bf16[128,640]{1,0:T(8,128)(2,1)S(1)}, bf16[128,640]{1,0:T(8,128)(2,1)S(1)}, u32[]{:S(2)}, u32[]{:S(2)}) collective-permute-start(bf16[128,640]{1,0:T(8,128)(2,1)S(1)} %get-tuple-element.12), channel_id=1, source_target_pairs={{0,16},{16,32},{32,48},{48,64},{64,80},{80,96},{96,112},{112,128},... | collective-permute-start | bytes 491528 | tf_op jit(solution)/shard_map/ppermute | solution.py:16
  109.8 52.9 %copy-start.5 = (bf16[128,640]{1,0:T(8,128)(2,1)S(1)}, bf16[128,640]{1,0:T(8,128)(2,1)}, u32[]{:S(2)}) copy-start(bf16[128,640]{1,0:T(8,128)(2,1)} %fusion.115) | copy-start | bytes 491524
  109.8 116.9 %all-gather.9.cloned.1.call-start = ((), (), s32[]{:S(2)}) async-start(), calls=%async_computation.1 | async-start | bytes 1474560 | tf_op jit(solution)/shard_map/all_gather | solution.py:60
  109.9 61.6 %collective-permute-start.3 = (bf16[128,5]{0,1:T(8,128)(2,1)S(1)}, bf16[128,5]{0,1:T(8,128)(2,1)S(1)}, u32[]{:S(2)}, u32[]{:S(2)}) collective-permute-start(bf16[128,5]{0,1:T(8,128)(2,1)S(1)} %bitcast.139), channel_id=1, source_target_pairs={{0,16},{16,32},{32,48},{48,64},{64,80},{80,96},{96,112},{112,128},... | collective-permute-start | bytes 3848 | tf_op jit(solution)/shard_map/ppermute | solution.py:16
  159.1 3.5 %copy-start.2 = (bf16[128,5120]{1,0:T(8,128)(2,1)S(1)}, bf16[128,5120]{1,0:T(8,128)(2,1)}, u32[]{:S(2)}) copy-start(bf16[128,5120]{1,0:T(8,128)(2,1)} %all-gather.7.cloned.1.call-done) | copy-start | bytes 3932164
  166.9 10.8 %collective-permute-start.2 = (bf16[128,640]{1,0:T(8,128)(2,1)S(1)}, bf16[128,640]{1,0:T(8,128)(2,1)S(1)}, u32[]{:S(2)}, u32[]{:S(2)}) collective-permute-start(bf16[128,640]{1,0:T(8,128)(2,1)S(1)} %get-tuple-element.14), channel_id=1, source_target_pairs={{0,16},{16,32},{32,48},{48,64},{64,80},{80,96},{96,112},{112,128},... | collective-permute-start | bytes 491528 | tf_op jit(solution)/shard_map/ppermute | solution.py:16
  178.5 51.7 %copy-start.6 = (bf16[128,640]{1,0:T(8,128)(2,1)S(1)}, bf16[128,640]{1,0:T(8,128)(2,1)}, u32[]{:S(2)}) copy-start(bf16[128,640]{1,0:T(8,128)(2,1)} %fusion.116) | copy-start | bytes 491524
  178.5 60.5 %collective-permute-start.5 = (bf16[128,5]{0,1:T(8,128)(2,1)S(1)}, bf16[128,5]{0,1:T(8,128)(2,1)S(1)}, u32[]{:S(2)}, u32[]{:S(2)}) collective-permute-start(bf16[128,5]{0,1:T(8,128)(2,1)S(1)} %bitcast.140), channel_id=1, source_target_pairs={{0,16},{16,32},{32,48},{48,64},{64,80},{80,96},{96,112},{112,128},... | collective-permute-start | bytes 3848 | tf_op jit(solution)/shard_map/ppermute | solution.py:16
  226.7 3.5 %copy-start.3 = (bf16[128,5120]{1,0:T(8,128)(2,1)S(1)}, bf16[128,5120]{1,0:T(8,128)(2,1)}, u32[]{:S(2)}) copy-start(bf16[128,5120]{1,0:T(8,128)(2,1)} %all-gather.9.cloned.1.call-done) | copy-start | bytes 3932164
  234.4 10.8 %collective-permute-start.4 = (bf16[128,640]{1,0:T(8,128)(2,1)S(1)}, bf16[128,640]{1,0:T(8,128)(2,1)S(1)}, u32[]{:S(2)}, u32[]{:S(2)}) collective-permute-start(bf16[128,640]{1,0:T(8,128)(2,1)S(1)} %get-tuple-element.16), channel_id=1, source_target_pairs={{0,16},{16,32},{32,48},{48,64},{64,80},{80,96},{96,112},{112,128},... | collective-permute-start | bytes 491528 | tf_op jit(solution)/shard_map/ppermute | solution.py:16
Sparse Core Ops, SparseCore 0:
  10.1 52.3 all-gather.10
  64.6 28.1 all-gather.12
  109.9 49.1 all-gather.6
  178.6 47.9 all-gather.8
where the time goes:
time: 253 us; the launch traced here: 252 us
  waiting for transfers between devices  184 us (73%)
  starting transfers between devices  21.8 us (9%)
  other arithmetic  14.4 us (6%)
  between operations  14.3 us (6%)
  matrix products  12.6 us (5%)
  local copies, waits for them, and re-layouts  4.92 us (2%)
    all_gather x3, waiting for transfers between devices, shards(): full_rows = lax.all_gather(current, 'tensor', axis=1, tiled=True)  138 us
    all_gather x1, waiting for transfers between devices, shards(): weight_all = lax.all_gather(weight_local, 'dp', axis=0, tiled=True)  26.8 us
    ppermute x6, starting transfers between devices, from_behind(): lax.ppermute(value, axis, [(source, source + steps) for source in range(f...  21.6 us
    ppermute x6, waiting for transfers between devices, from_behind(): lax.ppermute(value, axis, [(source, source + steps) for source in range(f...  18.8 us
    dot_general x3, matrix products, shards(): projected = jnp.dot(normed, weight_all, preferred_element_type=jnp.float32)  12.6 us
    reduce_sum x3, other arithmetic, normalize(): spread = jnp.mean(centered * centered, axis=-1, keepdims=True)  5.45 us
    reduce_sum x3, other arithmetic, normalize(): average = jnp.mean(values, axis=-1, keepdims=True)  5.06 us
  transfers between devices with their start and end apart: 10, of which 7 were waited for; matrix products, arithmetic and copies ran while one was open for 12% of the time, Pallas kernels for 0%

commit v1 on v0

v1 whole, which is shorter than its diff:
```python
import functools

import jax
import jax.numpy as jnp
from jax import lax
from jax.experimental import pallas as pl
from jax.experimental.pallas import tpu as pltpu
from jax.sharding import PartitionSpec as P

TICKS = 3

norm_eps = 1e-05
clip_limit = 4.0
LANES = 128
VMEM_LIMIT = 16 * 1024 * 1024


def tick_kernel(
    step,
    ids,
    gathered,
    w_own,
    w_other,
    base_out,
    base_in,
    fresh,
    gain_far,
    shift_far,
    bias_far,
    exps_far,
    result,
    sent,
    held,
    normed,
    base,
    gain,
    shift,
    bias,
    exps,
    sem,
    load_sem,
):
    peers, rows, cols = gathered.shape
    seq = base_out.shape[1]
    seqs = rows // seq
    per_half = normed.shape[2] // cols
    tiles = [(peer, col) for peer in range(peers) for col in range(0, cols, LANES)]
    width = float(peers * cols)
    section = lax.axis_index("section")
    own = lax.axis_index("dp")
    mine = lax.axis_index("tensor")
    batch = step + lax.axis_size("section") - 1 - section
    arriving_batch = jnp.minimum(batch + 1, ids.shape[1] - 1)

    loads = [
        pltpu.make_async_copy(source, target, load_sem.at[load_no])
        for load_no, (source, target) in enumerate(
            [(gain_far, gain), (shift_far, shift), (bias_far, bias), (exps_far, exps)]
        )
    ]
    for load in loads:
        load.start()
    bases = []
    for seq_no in range(seqs):
        low = seq_no * seq
        place = pl.ds(low, seq)
        bases.append(
            pltpu.make_async_copy(
                base_out.at[ids[seq_no, batch]], base.at[place], sem.at[seq_no]
            )
        )
        bases[-1].start()
        in_slot = ids[seq_no, arriving_batch]

        @pl.when(section > 0)
        def _():
            pltpu.make_async_copy(
                base_in.at[in_slot], held.at[place], sem.at[seqs + seq_no]
            ).start()

        if step < fresh.shape[0]:

            @pl.when(section == 0)
            def _():
                pltpu.make_async_copy(
                    fresh.at[step, place], held.at[place], sem.at[seqs + seq_no]
                ).start()

    total = jnp.zeros((rows, LANES), jnp.float32)
    for peer, col in tiles:
        total += gathered[peer, :, col : col + LANES].astype(jnp.float32)
    average = jnp.sum(total, axis=-1, keepdims=True) / width
    total = jnp.zeros((rows, LANES), jnp.float32)
    for peer, col in tiles:
        centered = gathered[peer, :, col : col + LANES].astype(jnp.float32) - average
        total += centered * centered
    scale = lax.rsqrt(jnp.sum(total, axis=-1, keepdims=True) / width + norm_eps)
    for load in loads:
        load.wait()
    for peer, col in tiles:
        at = peer * cols + col
        centered = gathered[peer, :, col : col + LANES].astype(jnp.float32) - average
        value = centered * scale * gain[:, at : at + LANES] + shift[:, at : at + LANES]
        start = (peer % per_half) * cols + col
        normed[peer // per_half, :, start : start + LANES] = value.astype(jnp.bfloat16)

    projected = jnp.dot(normed[own], w_own[...], preferred_element_type=jnp.float32)
    projected += jnp.dot(normed[1 - own], w_other[...], preferred_element_type=jnp.float32)
    relu = jnp.maximum(projected + bias[...], 0.0)
    result[...] = (gathered[mine].astype(jnp.float32) + relu).astype(jnp.bfloat16)
    for copy in bases:
        copy.wait()
    for block in range(cols // LANES):
        top = clip_limit * jnp.exp2(exps[step, block].astype(jnp.float32))
        top = jnp.transpose(jnp.broadcast_to(top, (LANES, rows)))
        span = slice(block * LANES, (block + 1) * LANES)
        delta = result[:, span].astype(jnp.float32) - base[:, span].astype(jnp.float32)
        sent[:, span] = jnp.clip(delta, -top, top).astype(jnp.bfloat16)
    for seq_no in range(seqs):
        landed = pltpu.make_async_copy(
            base_in.at[0], held.at[pl.ds(seq_no * seq, seq)], sem.at[seqs + seq_no]
        )
        if step < fresh.shape[0]:
            landed.wait()
        else:

            @pl.when(section > 0)
            def _():
                landed.wait()

            @pl.when(section == 0)
            def _():
                held[seq_no * seq : (seq_no + 1) * seq] = jnp.zeros((seq, cols), jnp.bfloat16)


def copies_kernel(source, copies, held, sem):
    load = pltpu.make_async_copy(source, held, sem)
    load.start()
    load.wait()
    for peer in range(copies.shape[0]):
        copies[peer] = held[...]


def rebuild_kernel(held, arriving, copies):
    total = held[...].astype(jnp.float32) + arriving[...].astype(jnp.float32)
    rebuilt = total.astype(jnp.bfloat16)
    for peer in range(copies.shape[0]):
        copies[peer] = rebuilt


VMEM = pl.BlockSpec(memory_space=pltpu.VMEM)
SMEM = pl.BlockSpec(memory_space=pltpu.SMEM)
HBM = pl.BlockSpec(memory_space=pltpu.HBM)


def in_hbm(*arrays):
    return [pltpu.with_memory_space_constraint(array, pltpu.HBM) for array in arrays]


def tick(step, ids, gathered, gain, shift, bias, w_own, w_other, base_out, base_in, fresh, exps):
    peers, rows, cols = gathered.shape
    depth = w_own.shape[0]
    seqs = rows // base_out.shape[1]
    out = jax.ShapeDtypeStruct((rows, cols), jnp.bfloat16)
    return pl.pallas_call(
        functools.partial(tick_kernel, step),
        out_shape=(out, out, out),
        in_specs=[SMEM] + [VMEM] * 3 + [HBM] * 7,
        out_specs=(VMEM,) * 3,
        scratch_shapes=[
            pltpu.VMEM((2, rows, depth), jnp.bfloat16),
            pltpu.VMEM((rows, cols), jnp.bfloat16),
            pltpu.VMEM(gain.shape, jnp.float32),
            pltpu.VMEM(shift.shape, jnp.float32),
            pltpu.VMEM(bias.shape, jnp.float32),
            pltpu.VMEM(exps.shape, jnp.int32),
            pltpu.SemaphoreType.DMA((2 * seqs,)),
            pltpu.SemaphoreType.DMA((4,)),
        ],
        compiler_params=pltpu.CompilerParams(vmem_limit_bytes=VMEM_LIMIT),
        cost_estimate=pl.CostEstimate(
            flops=4 * rows * depth * cols, bytes_accessed=4 * depth * cols, transcendentals=0
        ),
        name="tick",
    )(ids, gathered, w_own, w_other, *in_hbm(base_out, base_in, fresh, gain, shift, bias, exps))


def copies_of(block, peers):
    rows, cols = block.shape
    return pl.pallas_call(
        copies_kernel,
        out_shape=jax.ShapeDtypeStruct((peers, rows, cols), jnp.bfloat16),
        in_specs=[HBM],
        out_specs=VMEM,
        scratch_shapes=[pltpu.VMEM((rows, cols), jnp.bfloat16), pltpu.SemaphoreType.DMA(())],
        compiler_params=pltpu.CompilerParams(vmem_limit_bytes=VMEM_LIMIT),
        cost_estimate=pl.CostEstimate(
            flops=0, bytes_accessed=2 * (peers + 1) * rows * cols, transcendentals=0
        ),
        name="copies",
    )(*in_hbm(block))


def rebuild(peers, held, arriving):
    rows, cols = arriving.shape
    return pl.pallas_call(
        rebuild_kernel,
        out_shape=jax.ShapeDtypeStruct((peers, rows, cols), jnp.bfloat16),
        in_specs=[VMEM, VMEM],
        out_specs=VMEM,
        compiler_params=pltpu.CompilerParams(vmem_limit_bytes=VMEM_LIMIT),
        cost_estimate=pl.CostEstimate(
            flops=2 * rows * cols, bytes_accessed=2 * (peers + 2) * rows * cols, transcendentals=0
        ),
        name="rebuild",
    )(held, arriving)


def shards(
    start_acts,
    fresh_acts,
    ln_gain,
    ln_shift,
    proj,
    proj_bias,
    sample_ids,
    base_out,
    base_in,
    scale_exps,
):
    sections = lax.axis_size("section")
    peers = lax.axis_size("tensor")
    forward = [(source, source + 1) for source in range(sections - 1)]
    w_own = proj[0]
    w_other = lax.ppermute(w_own, "dp", [(0, 1), (1, 0)])
    ids = jnp.transpose(sample_ids)
    exps = jnp.transpose(scale_exps, (1, 3, 0, 2))
    copies = copies_of(start_acts[0], peers)
    outputs = []
    for step in range(TICKS):
        gathered = lax.all_to_all(copies, "tensor", 0, 0)
        result, sent, held = tick(
            step, ids, gathered, ln_gain, ln_shift, proj_bias, w_own, w_other, base_out[0], base_in[0],
            fresh_acts, exps,
        )
        outputs.append(result)
        arriving = lax.ppermute(sent, "section", forward)
        copies = rebuild(peers if step + 1 < TICKS else 1, held, arriving)
    return (jnp.stack(outputs, axis=0)[None], copies)


def solution(mesh):
    return jax.shard_map(
        shards,
        mesh=mesh,
        in_specs=(
            P("section", "dp", "tensor"),
            P(None, "dp", "tensor"),
            P("section", None),
            P("section", None),
            P("section", "dp", "tensor"),
            P("section", "tensor"),
            P(None, "dp"),
            P("section", "dp", None, "tensor"),
            P("section", "dp", None, "tensor"),
            P("section", None, "dp", "tensor"),
        ),
        out_specs=(P("section", None, "dp", "tensor"), P("section", "dp", "tensor")),
        check_vma=False,
    )
```

time: 253 us -> 110 us (0.43)
  the two profiles are of different devices: /device:TPU:136 before, /device:TPU:384 now
where the time goes in v1:
time: 110 us; the launch traced here: 109 us
  blocking collectives  61.8 us (56%)
  waiting for transfers between devices  22.4 us (20%)
  Pallas kernels  12.1 us (11%)
  starting transfers between devices  11.3 us (10%)
    all_to_all x3, blocking collectives, shards(): gathered = lax.all_to_all(copies, 'tensor', 0, 0)  61.8 us
    ppermute x3, waiting for transfers between devices, shards(): arriving = lax.ppermute(sent, 'section', forward)  22.4 us
    pallas_call x3, Pallas kernels, tick(): pl.pallas_call(functools.partial(tick_kernel, step), out_shape=(out, out,...  9.97 us
    ppermute x3, starting transfers between devices, shards(): arriving = lax.ppermute(sent, 'section', forward)  9.43 us
  transfers between devices with their start and end apart: 4, of which 3 were waited for; matrix products, arithmetic and copies ran while one was open for 1% of the time, Pallas kernels for 1%

profile of v1, /device:TPU:384, one launch (start us, length us, event | category | flops | bytes accessed | tf_op | source)
XLA Modules:
  0.0 109.2 jit_solution(13246547205838876405)
XLA Ops:
  0.6 1.9 %collective-permute-start = (bf16[2560,640]{1,0:T(8,128)(2,1)}, bf16[2560,640]{1,0:T(8,128)(2,1)S(1)}, u32[]{:S(2)}, u32[]{:S(2)}) collective-permute-start(bf16[2560,640]{1,0:T(8,128)(2,1)} %bitcast.11), channel_id=1, source_target_pairs={{0,1},{1,0},{2,3},{3,2},{4,5},{5,4},{6,7},{7,6},{8,9},{9,8},{10,11... | collective-permute-start | bytes 9830408 | tf_op jit(solution)/shard_map/ppermute | solution.py:235
  2.6 0.0 copy-start
  2.6 1.2 %copies.1 = bf16[8,128,640]{2,1,0:T(8,128)(2,1)S(1)} custom-call(bf16[128,640]{1,0:T(8,128)(2,1)} %bitcast.27), custom_call_target="tpu_custom_call" | custom-call | bytes 1474560 | tf_op jit(solution)/shard_map/copies/pallas_call | solution.py:190
  3.8 0.0 copy-start.1
  3.8 23.9 %all_to_all.15.gathered = bf16[8,128,640]{2,1,0:T(8,128)(2,1)S(1)} all-to-all(bf16[8,128,640]{2,1,0:T(8,128)(2,1)S(1)} %copies.1), channel_id=1, replica_groups=mesh['section'=32,'tensor'=8,'dp'=2] {'tensor'}, dimensions={0} | all-to-all | bytes 2621440 | tf_op jit(solution)/shard_map/all_to_all | solution.py:241
  27.7 0.0 collective-permute-done.w_other
  27.7 0.0 copy-done
  27.7 0.0 copy-done.1
  27.7 3.3 %tick.3 = (bf16[128,640]{1,0:T(8,128)(2,1)S(1)}, bf16[128,640]{1,0:T(8,128)(2,1)S(1)}, bf16[128,640]{1,0:T(8,128)(2,1)S(1)}) custom-call(s32[2,34]{1,0:T(2,128)S(1)} %bitcast.18, bf16[8,128,640]{2,1,0:T(8,128)(2,1)S(1)} %all_to_all.15.gathered, bf16[2560,640]{1,0:T(8,128)(2,1)S(1)} %bitcast.12, bf16[2560,640]{1,0:T(8,128)(2,1)S(1)} %collective-permute-done.w_other, ...), custom_call_target="tpu_custom_call" | custom-call | flops 838860800 | bytes 6553600 | tf_op jit(solution)/shard_map/tick/pallas_call | solution.py:165
  31.1 4.8 %collective-permute-start.1 = (bf16[128,640]{1,0:T(8,128)(2,1)S(1)}, bf16[128,640]{1,0:T(8,128)(2,1)S(1)}, u32[]{:S(2)}, u32[]{:S(2)}) collective-permute-start(bf16[128,640]{1,0:T(8,128)(2,1)S(1)} %get-tuple-element.13), channel_id=1, source_target_pairs={{0,16},{16,32},{32,48},{48,64},{64,80},{80,96},{96,112},{112,128},... | collective-permute-start | bytes 491528 | tf_op jit(solution)/shard_map/ppermute | solution.py:247
  35.9 6.2 %collective-permute-done.1.arriving = bf16[128,640]{1,0:T(8,128)(2,1)S(1)} collective-permute-done((bf16[128,640]{1,0:T(8,128)(2,1)S(1)}, bf16[128,640]{1,0:T(8,128)(2,1)S(1)}, u32[]{:S(2)}, u32[]{:S(2)}) %collective-permute-start.1) | collective-permute-done | bytes 163872 | tf_op jit(solution)/shard_map/ppermute | solution.py:247
  42.0 0.1 rebuild.3
  42.1 20.1 %all_to_all.16.gathered = bf16[8,128,640]{2,1,0:T(8,128)(2,1)S(1)} all-to-all(bf16[8,128,640]{2,1,0:T(8,128)(2,1)S(1)} %rebuild.3), channel_id=1, replica_groups=mesh['section'=32,'tensor'=8,'dp'=2] {'tensor'}, dimensions={0} | all-to-all | bytes 2621440 | tf_op jit(solution)/shard_map/all_to_all | solution.py:241
  62.2 3.3 %tick.4 = (bf16[128,640]{1,0:T(8,128)(2,1)S(1)}, bf16[128,640]{1,0:T(8,128)(2,1)S(1)}, bf16[128,640]{1,0:T(8,128)(2,1)S(1)}) custom-call(s32[2,34]{1,0:T(2,128)S(1)} %bitcast.19, bf16[8,128,640]{2,1,0:T(8,128)(2,1)S(1)} %all_to_all.16.gathered, bf16[2560,640]{1,0:T(8,128)(2,1)S(1)} %bitcast.13, bf16[2560,640]{1,0:T(8,128)(2,1)S(1)} %collective-permute-done.w_other, ...), custom_call_target="tpu_custom_call" | custom-call | flops 838860800 | bytes 6553600 | tf_op jit(solution)/shard_map/tick/pallas_call | solution.py:165
  65.5 2.7 %collective-permute-start.2 = (bf16[128,640]{1,0:T(8,128)(2,1)S(1)}, bf16[128,640]{1,0:T(8,128)(2,1)S(1)}, u32[]{:S(2)}, u32[]{:S(2)}) collective-permute-start(bf16[128,640]{1,0:T(8,128)(2,1)S(1)} %get-tuple-element.16), channel_id=1, source_target_pairs={{0,16},{16,32},{32,48},{48,64},{64,80},{80,96},{96,112},{112,128},... | collective-permute-start | bytes 491528 | tf_op jit(solution)/shard_map/ppermute | solution.py:247
  68.2 8.2 %collective-permute-done.2.arriving = bf16[128,640]{1,0:T(8,128)(2,1)S(1)} collective-permute-done((bf16[128,640]{1,0:T(8,128)(2,1)S(1)}, bf16[128,640]{1,0:T(8,128)(2,1)S(1)}, u32[]{:S(2)}, u32[]{:S(2)}) %collective-permute-start.2) | collective-permute-done | bytes 163872 | tf_op jit(solution)/shard_map/ppermute | solution.py:247
  76.4 0.1 rebuild.4
  76.6 17.8 %all_to_all.17.gathered = bf16[8,128,640]{2,1,0:T(8,128)(2,1)S(1)} all-to-all(bf16[8,128,640]{2,1,0:T(8,128)(2,1)S(1)} %rebuild.4), channel_id=1, replica_groups=mesh['section'=32,'tensor'=8,'dp'=2] {'tensor'}, dimensions={0} | all-to-all | bytes 2621440 | tf_op jit(solution)/shard_map/all_to_all | solution.py:241
  94.4 3.3 %tick.5 = (bf16[128,640]{1,0:T(8,128)(2,1)S(1)}, bf16[128,640]{1,0:T(8,128)(2,1)S(1)}, bf16[128,640]{1,0:T(8,128)(2,1)S(1)}) custom-call(s32[2,34]{1,0:T(2,128)S(1)} %bitcast.20, bf16[8,128,640]{2,1,0:T(8,128)(2,1)S(1)} %all_to_all.17.gathered, bf16[2560,640]{1,0:T(8,128)(2,1)S(1)} %bitcast.14, bf16[2560,640]{1,0:T(8,128)(2,1)S(1)} %collective-permute-done.w_other, ...), custom_call_target="tpu_custom_call" | custom-call | flops 838860800 | bytes 6553600 | tf_op jit(solution)/shard_map/tick/pallas_call | solution.py:165
  97.7 1.9 %collective-permute-start.3 = (bf16[128,640]{1,0:T(8,128)(2,1)S(1)}, bf16[128,640]{1,0:T(8,128)(2,1)S(1)}, u32[]{:S(2)}, u32[]{:S(2)}) collective-permute-start(bf16[128,640]{1,0:T(8,128)(2,1)S(1)} %get-tuple-element.19), channel_id=1, source_target_pairs={{0,16},{16,32},{32,48},{48,64},{64,80},{80,96},{96,112},{112,128},... | collective-permute-start | bytes 491528 | tf_op jit(solution)/shard_map/ppermute | solution.py:247
  99.6 0.8 maximum_bitcast_fusion
  100.5 8.1 %collective-permute-done.3.arriving = bf16[128,640]{1,0:T(8,128)(2,1)S(1)} collective-permute-done((bf16[128,640]{1,0:T(8,128)(2,1)S(1)}, bf16[128,640]{1,0:T(8,128)(2,1)S(1)}, u32[]{:S(2)}, u32[]{:S(2)}) %collective-permute-start.3) | collective-permute-done | bytes 163872 | tf_op jit(solution)/shard_map/ppermute | solution.py:247
  108.5 0.7 rebuild.5
Async XLA Ops:
  0.6 27.1 %collective-permute-start = (bf16[2560,640]{1,0:T(8,128)(2,1)}, bf16[2560,640]{1,0:T(8,128)(2,1)S(1)}, u32[]{:S(2)}, u32[]{:S(2)}) collective-permute-start(bf16[2560,640]{1,0:T(8,128)(2,1)} %bitcast.11), channel_id=1, source_target_pairs={{0,1},{1,0},{2,3},{3,2},{4,5},{5,4},{6,7},{7,6},{8,9},{9,8},{10,11... | collective-permute-start | bytes 9830408 | tf_op jit(solution)/shard_map/ppermute | solution.py:235
  2.6 25.1 %copy-start = (bf16[1,2560,640]{2,1,0:T(8,128)(2,1)S(1)}, bf16[1,2560,640]{2,1,0:T(8,128)(2,1)}, u32[]{:S(2)}) copy-start(bf16[1,2560,640]{2,1,0:T(8,128)(2,1)} %param.14) | copy-start | bytes 9830404
  3.8 24.0 %copy-start.1 = (s32[34,2]{0,1:T(2,128)S(1)}, s32[34,2]{0,1:T(2,128)}, u32[]{:S(2)}) copy-start(s32[34,2]{0,1:T(2,128)} %param.16) | copy-start | bytes 820
  31.1 11.0 %collective-permute-start.1 = (bf16[128,640]{1,0:T(8,128)(2,1)S(1)}, bf16[128,640]{1,0:T(8,128)(2,1)S(1)}, u32[]{:S(2)}, u32[]{:S(2)}) collective-permute-start(bf16[128,640]{1,0:T(8,128)(2,1)S(1)} %get-tuple-element.13), channel_id=1, source_target_pairs={{0,16},{16,32},{32,48},{48,64},{64,80},{80,96},{96,112},{112,128},... | collective-permute-start | bytes 491528 | tf_op jit(solution)/shard_map/ppermute | solution.py:247
  65.5 10.9 %collective-permute-start.2 = (bf16[128,640]{1,0:T(8,128)(2,1)S(1)}, bf16[128,640]{1,0:T(8,128)(2,1)S(1)}, u32[]{:S(2)}, u32[]{:S(2)}) collective-permute-start(bf16[128,640]{1,0:T(8,128)(2,1)S(1)} %get-tuple-element.16), channel_id=1, source_target_pairs={{0,16},{16,32},{32,48},{48,64},{64,80},{80,96},{96,112},{112,128},... | collective-permute-start | bytes 491528 | tf_op jit(solution)/shard_map/ppermute | solution.py:247
  97.7 10.8 %collective-permute-start.3 = (bf16[128,640]{1,0:T(8,128)(2,1)S(1)}, bf16[128,640]{1,0:T(8,128)(2,1)S(1)}, u32[]{:S(2)}, u32[]{:S(2)}) collective-permute-start(bf16[128,640]{1,0:T(8,128)(2,1)S(1)} %get-tuple-element.19), channel_id=1, source_target_pairs={{0,16},{16,32},{32,48},{48,64},{64,80},{80,96},{96,112},{112,128},... | collective-permute-start | bytes 491528 | tf_op jit(solution)/shard_map/ppermute | solution.py:247

commit v2 on v1

--- a/solution.py
+++ b/solution.py
@@ -32,6 +32,7 @@
     sent,
     held,
     normed,
+    projected,
     base,
     gain,
     shift,
@@ -97,16 +98,31 @@
     scale = lax.rsqrt(jnp.sum(total, axis=-1, keepdims=True) / width + norm_eps)
     for load in loads:
         load.wait()
-    for peer, col in tiles:
-        at = peer * cols + col
-        centered = gathered[peer, :, col : col + LANES].astype(jnp.float32) - average
-        value = centered * scale * gain[:, at : at + LANES] + shift[:, at : at + LANES]
-        start = (peer % per_half) * cols + col
-        normed[peer // per_half, :, start : start + LANES] = value.astype(jnp.bfloat16)
-
-    projected = jnp.dot(normed[own], w_own[...], preferred_element_type=jnp.float32)
-    projected += jnp.dot(normed[1 - own], w_other[...], preferred_element_type=jnp.float32)
-    relu = jnp.maximum(projected + bias[...], 0.0)
+
+    def norm_half(half):
+        for peer, col in tiles[half * len(tiles) // 2 : (half + 1) * len(tiles) // 2]:
+            at = peer * cols + col
+            centered = gathered[peer, :, col : col + LANES].astype(jnp.float32) - average
+            value = centered * scale * gain[:, at : at + LANES] + shift[:, at : at + LANES]
+            start = (peer % per_half) * cols + col
+            normed[half, :, start : start + LANES] = value.astype(jnp.bfloat16)
+
+    def project(first, second):
+        norm_half(0)
+        low = jnp.dot(normed[0], first[...], preferred_element_type=jnp.float32)
+        norm_half(1)
+        high = jnp.dot(normed[1], second[...], preferred_element_type=jnp.float32)
+        projected[...] = low + high + bias[...]
+
+    @pl.when(own == 0)
+    def _():
+        project(w_own, w_other)
+
+    @pl.when(own != 0)
+    def _():
+        project(w_other, w_own)
+
+    relu = jnp.maximum(projected[...], 0.0)
     result[...] = (gathered[mine].astype(jnp.float32) + relu).astype(jnp.bfloat16)
     for copy in bases:
         copy.wait()
@@ -133,12 +149,10 @@
                 held[seq_no * seq : (seq_no + 1) * seq] = jnp.zeros((seq, cols), jnp.bfloat16)
 
 
-def copies_kernel(source, copies, held, sem):
-    load = pltpu.make_async_copy(source, held, sem)
-    load.start()
-    load.wait()
+def copies_kernel(source, copies):
+    block = source[...]
     for peer in range(copies.shape[0]):
-        copies[peer] = held[...]
+        copies[peer] = block
 
 
 def rebuild_kernel(held, arriving, copies):
@@ -169,6 +183,7 @@
         out_specs=(VMEM,) * 3,
         scratch_shapes=[
             pltpu.VMEM((2, rows, depth), jnp.bfloat16),
+            pltpu.VMEM((rows, cols), jnp.float32),
             pltpu.VMEM((rows, cols), jnp.bfloat16),
             pltpu.VMEM(gain.shape, jnp.float32),
             pltpu.VMEM(shift.shape, jnp.float32),
@@ -190,15 +205,14 @@
     return pl.pallas_call(
         copies_kernel,
         out_shape=jax.ShapeDtypeStruct((peers, rows, cols), jnp.bfloat16),
-        in_specs=[HBM],
+        in_specs=[VMEM],
         out_specs=VMEM,
-        scratch_shapes=[pltpu.VMEM((rows, cols), jnp.bfloat16), pltpu.SemaphoreType.DMA(())],
         compiler_params=pltpu.CompilerParams(vmem_limit_bytes=VMEM_LIMIT),
         cost_estimate=pl.CostEstimate(
             flops=0, bytes_accessed=2 * (peers + 1) * rows * cols, transcendentals=0
         ),
         name="copies",
-    )(*in_hbm(block))
+    )(block)
 
 
 def rebuild(peers, held, arriving):

time: 110 us -> 109 us (level)
  Pallas kernels: 12.1 us -> 10.4 us
  transfers between devices with their start and end apart: 4 -> 4, of which waited for: 3 -> 3; matrix products, arithmetic and copies ran while one was open for 1% -> 1% of each run, Pallas kernels for 1% -> 0%
where the time goes in v2:
time: 109 us
  blocking collectives  62.1 us (57%)
  waiting for transfers between devices  22.4 us (21%)
  starting transfers between devices  11.3 us (10%)
  Pallas kernels  10.4 us (10%)
    all_to_all x3, blocking collectives, shards(): gathered = lax.all_to_all(copies, 'tensor', 0, 0)  62.1 us
    ppermute x3, waiting for transfers between devices, shards(): arriving = lax.ppermute(sent, 'section', forward)  22.4 us
    ppermute x3, starting transfers between devices, shards(): arriving = lax.ppermute(sent, 'section', forward)  9.43 us
    pallas_call x3, Pallas kernels, tick(): pl.pallas_call(functools.partial(tick_kernel, step), out_shape=(out, out,...  9.37 us
  transfers between devices with their start and end apart: 4, of which 3 were waited for; matrix products, arithmetic and copies ran while one was open for 1% of the time, Pallas kernels for 0%

profile of v2, /device:TPU:384, one launch (start us, length us, event | category | flops | bytes accessed | tf_op | source)
XLA Modules:
  0.0 108.8 jit_solution(14255923598847819178)
XLA Ops:
  0.6 1.9 %collective-permute-start = (bf16[2560,640]{1,0:T(8,128)(2,1)}, bf16[2560,640]{1,0:T(8,128)(2,1)S(1)}, u32[]{:S(2)}, u32[]{:S(2)}) collective-permute-start(bf16[2560,640]{1,0:T(8,128)(2,1)} %bitcast.11), channel_id=1, source_target_pairs={{0,1},{1,0},{2,3},{3,2},{4,5},{5,4},{6,7},{7,6},{8,9},{9,8},{10,11... | collective-permute-start | bytes 9830408 | tf_op jit(solution)/shard_map/ppermute | solution.py:249
  2.6 0.0 copy-start.1
  2.6 0.9 copy-done.1
  3.5 0.1 copies.1
  3.6 0.0 copy-start.2
  3.6 24.2 %all_to_all.15.gathered = bf16[8,128,640]{2,1,0:T(8,128)(2,1)S(1)} all-to-all(bf16[8,128,640]{2,1,0:T(8,128)(2,1)S(1)} %copies.1), channel_id=1, replica_groups=mesh['section'=32,'tensor'=8,'dp'=2] {'tensor'}, dimensions={0} | all-to-all | bytes 2621440 | tf_op jit(solution)/shard_map/all_to_all | solution.py:255
  27.8 0.0 collective-permute-done.w_other
  27.8 0.0 copy-done
  27.8 0.0 copy-done.2
  27.8 3.1 %tick.3 = (bf16[128,640]{1,0:T(8,128)(2,1)S(1)}, bf16[128,640]{1,0:T(8,128)(2,1)S(1)}, bf16[128,640]{1,0:T(8,128)(2,1)S(1)}) custom-call(s32[2,34]{1,0:T(2,128)S(1)} %bitcast.19, bf16[8,128,640]{2,1,0:T(8,128)(2,1)S(1)} %all_to_all.15.gathered, bf16[2560,640]{1,0:T(8,128)(2,1)S(1)} %bitcast.12, bf16[2560,640]{1,0:T(8,128)(2,1)S(1)} %collective-permute-done.w_other, ...), custom_call_target="tpu_custom_call" | custom-call | flops 838860800 | bytes 6553600 | tf_op jit(solution)/shard_map/tick/pallas_call | solution.py:179
  30.9 4.8 %collective-permute-start.1 = (bf16[128,640]{1,0:T(8,128)(2,1)S(1)}, bf16[128,640]{1,0:T(8,128)(2,1)S(1)}, u32[]{:S(2)}, u32[]{:S(2)}) collective-permute-start(bf16[128,640]{1,0:T(8,128)(2,1)S(1)} %get-tuple-element.13), channel_id=1, source_target_pairs={{0,16},{16,32},{32,48},{48,64},{64,80},{80,96},{96,112},{112,128},... | collective-permute-start | bytes 491528 | tf_op jit(solution)/shard_map/ppermute | solution.py:261
  35.7 6.2 %collective-permute-done.1.arriving = bf16[128,640]{1,0:T(8,128)(2,1)S(1)} collective-permute-done((bf16[128,640]{1,0:T(8,128)(2,1)S(1)}, bf16[128,640]{1,0:T(8,128)(2,1)S(1)}, u32[]{:S(2)}, u32[]{:S(2)}) %collective-permute-start.1) | collective-permute-done | bytes 163872 | tf_op jit(solution)/shard_map/ppermute | solution.py:261
  41.9 0.1 rebuild.3
  42.0 20.1 %all_to_all.16.gathered = bf16[8,128,640]{2,1,0:T(8,128)(2,1)S(1)} all-to-all(bf16[8,128,640]{2,1,0:T(8,128)(2,1)S(1)} %rebuild.3), channel_id=1, replica_groups=mesh['section'=32,'tensor'=8,'dp'=2] {'tensor'}, dimensions={0} | all-to-all | bytes 2621440 | tf_op jit(solution)/shard_map/all_to_all | solution.py:255
  62.1 3.2 %tick.4 = (bf16[128,640]{1,0:T(8,128)(2,1)S(1)}, bf16[128,640]{1,0:T(8,128)(2,1)S(1)}, bf16[128,640]{1,0:T(8,128)(2,1)S(1)}) custom-call(s32[2,34]{1,0:T(2,128)S(1)} %bitcast.20, bf16[8,128,640]{2,1,0:T(8,128)(2,1)S(1)} %all_to_all.16.gathered, bf16[2560,640]{1,0:T(8,128)(2,1)S(1)} %bitcast.13, bf16[2560,640]{1,0:T(8,128)(2,1)S(1)} %collective-permute-done.w_other, ...), custom_call_target="tpu_custom_call" | custom-call | flops 838860800 | bytes 6553600 | tf_op jit(solution)/shard_map/tick/pallas_call | solution.py:179
  65.3 2.7 %collective-permute-start.2 = (bf16[128,640]{1,0:T(8,128)(2,1)S(1)}, bf16[128,640]{1,0:T(8,128)(2,1)S(1)}, u32[]{:S(2)}, u32[]{:S(2)}) collective-permute-start(bf16[128,640]{1,0:T(8,128)(2,1)S(1)} %get-tuple-element.16), channel_id=1, source_target_pairs={{0,16},{16,32},{32,48},{48,64},{64,80},{80,96},{96,112},{112,128},... | collective-permute-start | bytes 491528 | tf_op jit(solution)/shard_map/ppermute | solution.py:261
  68.0 8.2 %collective-permute-done.2.arriving = bf16[128,640]{1,0:T(8,128)(2,1)S(1)} collective-permute-done((bf16[128,640]{1,0:T(8,128)(2,1)S(1)}, bf16[128,640]{1,0:T(8,128)(2,1)S(1)}, u32[]{:S(2)}, u32[]{:S(2)}) %collective-permute-start.2) | collective-permute-done | bytes 163872 | tf_op jit(solution)/shard_map/ppermute | solution.py:261
  76.2 0.1 rebuild.4
  76.3 17.9 %all_to_all.17.gathered = bf16[8,128,640]{2,1,0:T(8,128)(2,1)S(1)} all-to-all(bf16[8,128,640]{2,1,0:T(8,128)(2,1)S(1)} %rebuild.4), channel_id=1, replica_groups=mesh['section'=32,'tensor'=8,'dp'=2] {'tensor'}, dimensions={0} | all-to-all | bytes 2621440 | tf_op jit(solution)/shard_map/all_to_all | solution.py:255
  94.2 3.1 %tick.5 = (bf16[128,640]{1,0:T(8,128)(2,1)S(1)}, bf16[128,640]{1,0:T(8,128)(2,1)S(1)}, bf16[128,640]{1,0:T(8,128)(2,1)S(1)}) custom-call(s32[2,34]{1,0:T(2,128)S(1)} %bitcast.21, bf16[8,128,640]{2,1,0:T(8,128)(2,1)S(1)} %all_to_all.17.gathered, bf16[2560,640]{1,0:T(8,128)(2,1)S(1)} %bitcast.14, bf16[2560,640]{1,0:T(8,128)(2,1)S(1)} %collective-permute-done.w_other, ...), custom_call_target="tpu_custom_call" | custom-call | flops 838860800 | bytes 6553600 | tf_op jit(solution)/shard_map/tick/pallas_call | solution.py:179
  97.3 1.9 %collective-permute-start.3 = (bf16[128,640]{1,0:T(8,128)(2,1)S(1)}, bf16[128,640]{1,0:T(8,128)(2,1)S(1)}, u32[]{:S(2)}, u32[]{:S(2)}) collective-permute-start(bf16[128,640]{1,0:T(8,128)(2,1)S(1)} %get-tuple-element.19), channel_id=1, source_target_pairs={{0,16},{16,32},{32,48},{48,64},{64,80},{80,96},{96,112},{112,128},... | collective-permute-start | bytes 491528 | tf_op jit(solution)/shard_map/ppermute | solution.py:261
  99.2 0.8 maximum_bitcast_fusion
  100.0 8.1 %collective-permute-done.3.arriving = bf16[128,640]{1,0:T(8,128)(2,1)S(1)} collective-permute-done((bf16[128,640]{1,0:T(8,128)(2,1)S(1)}, bf16[128,640]{1,0:T(8,128)(2,1)S(1)}, u32[]{:S(2)}, u32[]{:S(2)}) %collective-permute-start.3) | collective-permute-done | bytes 163872 | tf_op jit(solution)/shard_map/ppermute | solution.py:261
  108.1 0.7 rebuild.5
  (1 shorter events, 0.0 us)
Async XLA Ops:
  0.6 27.2 %collective-permute-start = (bf16[2560,640]{1,0:T(8,128)(2,1)}, bf16[2560,640]{1,0:T(8,128)(2,1)S(1)}, u32[]{:S(2)}, u32[]{:S(2)}) collective-permute-start(bf16[2560,640]{1,0:T(8,128)(2,1)} %bitcast.11), channel_id=1, source_target_pairs={{0,1},{1,0},{2,3},{3,2},{4,5},{5,4},{6,7},{7,6},{8,9},{9,8},{10,11... | collective-permute-start | bytes 9830408 | tf_op jit(solution)/shard_map/ppermute | solution.py:249
  2.6 0.9 copy-start.1
  3.5 24.3 %copy-start = (bf16[1,2560,640]{2,1,0:T(8,128)(2,1)S(1)}, bf16[1,2560,640]{2,1,0:T(8,128)(2,1)}, u32[]{:S(2)}) copy-start(bf16[1,2560,640]{2,1,0:T(8,128)(2,1)} %param.14) | copy-start | bytes 9830404
  3.6 24.2 %copy-start.2 = (s32[34,2]{0,1:T(2,128)S(1)}, s32[34,2]{0,1:T(2,128)}, u32[]{:S(2)}) copy-start(s32[34,2]{0,1:T(2,128)} %param.16) | copy-start | bytes 820
  30.9 11.0 %collective-permute-start.1 = (bf16[128,640]{1,0:T(8,128)(2,1)S(1)}, bf16[128,640]{1,0:T(8,128)(2,1)S(1)}, u32[]{:S(2)}, u32[]{:S(2)}) collective-permute-start(bf16[128,640]{1,0:T(8,128)(2,1)S(1)} %get-tuple-element.13), channel_id=1, source_target_pairs={{0,16},{16,32},{32,48},{48,64},{64,80},{80,96},{96,112},{112,128},... | collective-permute-start | bytes 491528 | tf_op jit(solution)/shard_map/ppermute | solution.py:261
  65.3 10.9 %collective-permute-start.2 = (bf16[128,640]{1,0:T(8,128)(2,1)S(1)}, bf16[128,640]{1,0:T(8,128)(2,1)S(1)}, u32[]{:S(2)}, u32[]{:S(2)}) collective-permute-start(bf16[128,640]{1,0:T(8,128)(2,1)S(1)} %get-tuple-element.16), channel_id=1, source_target_pairs={{0,16},{16,32},{32,48},{48,64},{64,80},{80,96},{96,112},{112,128},... | collective-permute-start | bytes 491528 | tf_op jit(solution)/shard_map/ppermute | solution.py:261
  97.3 10.8 %collective-permute-start.3 = (bf16[128,640]{1,0:T(8,128)(2,1)S(1)}, bf16[128,640]{1,0:T(8,128)(2,1)S(1)}, u32[]{:S(2)}, u32[]{:S(2)}) collective-permute-start(bf16[128,640]{1,0:T(8,128)(2,1)S(1)} %get-tuple-element.19), channel_id=1, source_target_pairs={{0,16},{16,32},{32,48},{48,64},{64,80},{80,96},{96,112},{112,128},... | collective-permute-start | bytes 491528 | tf_op jit(solution)/shard_map/ppermute | solution.py:261

commit v3 on v2

--- a/solution.py
+++ b/solution.py
@@ -87,15 +87,17 @@
                     fresh.at[step, place], held.at[place], sem.at[seqs + seq_no]
                 ).start()
 
+    near = gathered[0, :, :1].astype(jnp.float32)
     total = jnp.zeros((rows, LANES), jnp.float32)
+    squares = jnp.zeros((rows, LANES), jnp.float32)
     for peer, col in tiles:
-        total += gathered[peer, :, col : col + LANES].astype(jnp.float32)
-    average = jnp.sum(total, axis=-1, keepdims=True) / width
-    total = jnp.zeros((rows, LANES), jnp.float32)
-    for peer, col in tiles:
-        centered = gathered[peer, :, col : col + LANES].astype(jnp.float32) - average
-        total += centered * centered
-    scale = lax.rsqrt(jnp.sum(total, axis=-1, keepdims=True) / width + norm_eps)
+        offset = gathered[peer, :, col : col + LANES].astype(jnp.float32) - near
+        total += offset
+        squares += offset * offset
+    shifted = jnp.sum(total, axis=-1, keepdims=True) / width
+    spread = jnp.sum(squares, axis=-1, keepdims=True) / width - shifted * shifted
+    average = near + shifted
+    scale = lax.rsqrt(jnp.maximum(spread, 0.0) + norm_eps)
     for load in loads:
         load.wait()
 

time: 109 us -> 109 us (level)
  no operation moved by 1% of the time
where the time goes in v3:
time: 109 us
  blocking collectives  62.1 us (57%)
  waiting for transfers between devices  22.4 us (21%)
  starting transfers between devices  11.3 us (10%)
  Pallas kernels  10.5 us (10%)
    all_to_all x3, blocking collectives, shards(): gathered = lax.all_to_all(copies, 'tensor', 0, 0)  62.1 us
    ppermute x3, waiting for transfers between devices, shards(): arriving = lax.ppermute(sent, 'section', forward)  22.4 us
    pallas_call x3, Pallas kernels, tick(): pl.pallas_call(functools.partial(tick_kernel, step), out_shape=(out, out,...  9.51 us
    ppermute x3, starting transfers between devices, shards(): arriving = lax.ppermute(sent, 'section', forward)  9.43 us
  transfers between devices with their start and end apart: 4, of which 3 were waited for; matrix products, arithmetic and copies ran while one was open for 1% of the time, Pallas kernels for 0%

profile of v3, /device:TPU:384, one launch (start us, length us, event | category | flops | bytes accessed | tf_op | source)
XLA Modules:
  0.0 108.9 jit_solution(9041361280682530970)
XLA Ops:
  0.6 1.9 %collective-permute-start = (bf16[2560,640]{1,0:T(8,128)(2,1)}, bf16[2560,640]{1,0:T(8,128)(2,1)S(1)}, u32[]{:S(2)}, u32[]{:S(2)}) collective-permute-start(bf16[2560,640]{1,0:T(8,128)(2,1)} %bitcast.11), channel_id=1, source_target_pairs={{0,1},{1,0},{2,3},{3,2},{4,5},{5,4},{6,7},{7,6},{8,9},{9,8},{10,11... | collective-permute-start | bytes 9830408 | tf_op jit(solution)/shard_map/ppermute | solution.py:251
  2.6 0.0 copy-start.1
  2.6 0.9 copy-done.1
  3.5 0.1 copies.1
  3.6 0.0 copy-start.2
  3.6 24.2 %all_to_all.15.gathered = bf16[8,128,640]{2,1,0:T(8,128)(2,1)S(1)} all-to-all(bf16[8,128,640]{2,1,0:T(8,128)(2,1)S(1)} %copies.1), channel_id=1, replica_groups=mesh['section'=32,'tensor'=8,'dp'=2] {'tensor'}, dimensions={0} | all-to-all | bytes 2621440 | tf_op jit(solution)/shard_map/all_to_all | solution.py:257
  27.8 0.0 collective-permute-done.w_other
  27.8 0.0 copy-done
  27.8 0.0 copy-done.2
  27.8 3.2 %tick.3 = (bf16[128,640]{1,0:T(8,128)(2,1)S(1)}, bf16[128,640]{1,0:T(8,128)(2,1)S(1)}, bf16[128,640]{1,0:T(8,128)(2,1)S(1)}) custom-call(s32[2,34]{1,0:T(2,128)S(1)} %bitcast.19, bf16[8,128,640]{2,1,0:T(8,128)(2,1)S(1)} %all_to_all.15.gathered, bf16[2560,640]{1,0:T(8,128)(2,1)S(1)} %bitcast.12, bf16[2560,640]{1,0:T(8,128)(2,1)S(1)} %collective-permute-done.w_other, ...), custom_call_target="tpu_custom_call" | custom-call | flops 838860800 | bytes 6553600 | tf_op jit(solution)/shard_map/tick/pallas_call | solution.py:181
  31.0 4.8 %collective-permute-start.1 = (bf16[128,640]{1,0:T(8,128)(2,1)S(1)}, bf16[128,640]{1,0:T(8,128)(2,1)S(1)}, u32[]{:S(2)}, u32[]{:S(2)}) collective-permute-start(bf16[128,640]{1,0:T(8,128)(2,1)S(1)} %get-tuple-element.13), channel_id=1, source_target_pairs={{0,16},{16,32},{32,48},{48,64},{64,80},{80,96},{96,112},{112,128},... | collective-permute-start | bytes 491528 | tf_op jit(solution)/shard_map/ppermute | solution.py:263
  35.8 6.2 %collective-permute-done.1.arriving = bf16[128,640]{1,0:T(8,128)(2,1)S(1)} collective-permute-done((bf16[128,640]{1,0:T(8,128)(2,1)S(1)}, bf16[128,640]{1,0:T(8,128)(2,1)S(1)}, u32[]{:S(2)}, u32[]{:S(2)}) %collective-permute-start.1) | collective-permute-done | bytes 163872 | tf_op jit(solution)/shard_map/ppermute | solution.py:263
  42.0 0.1 rebuild.3
  42.1 20.1 %all_to_all.16.gathered = bf16[8,128,640]{2,1,0:T(8,128)(2,1)S(1)} all-to-all(bf16[8,128,640]{2,1,0:T(8,128)(2,1)S(1)} %rebuild.3), channel_id=1, replica_groups=mesh['section'=32,'tensor'=8,'dp'=2] {'tensor'}, dimensions={0} | all-to-all | bytes 2621440 | tf_op jit(solution)/shard_map/all_to_all | solution.py:257
  62.1 3.2 %tick.4 = (bf16[128,640]{1,0:T(8,128)(2,1)S(1)}, bf16[128,640]{1,0:T(8,128)(2,1)S(1)}, bf16[128,640]{1,0:T(8,128)(2,1)S(1)}) custom-call(s32[2,34]{1,0:T(2,128)S(1)} %bitcast.20, bf16[8,128,640]{2,1,0:T(8,128)(2,1)S(1)} %all_to_all.16.gathered, bf16[2560,640]{1,0:T(8,128)(2,1)S(1)} %bitcast.13, bf16[2560,640]{1,0:T(8,128)(2,1)S(1)} %collective-permute-done.w_other, ...), custom_call_target="tpu_custom_call" | custom-call | flops 838860800 | bytes 6553600 | tf_op jit(solution)/shard_map/tick/pallas_call | solution.py:181
  65.3 2.7 %collective-permute-start.2 = (bf16[128,640]{1,0:T(8,128)(2,1)S(1)}, bf16[128,640]{1,0:T(8,128)(2,1)S(1)}, u32[]{:S(2)}, u32[]{:S(2)}) collective-permute-start(bf16[128,640]{1,0:T(8,128)(2,1)S(1)} %get-tuple-element.16), channel_id=1, source_target_pairs={{0,16},{16,32},{32,48},{48,64},{64,80},{80,96},{96,112},{112,128},... | collective-permute-start | bytes 491528 | tf_op jit(solution)/shard_map/ppermute | solution.py:263
  68.0 8.2 %collective-permute-done.2.arriving = bf16[128,640]{1,0:T(8,128)(2,1)S(1)} collective-permute-done((bf16[128,640]{1,0:T(8,128)(2,1)S(1)}, bf16[128,640]{1,0:T(8,128)(2,1)S(1)}, u32[]{:S(2)}, u32[]{:S(2)}) %collective-permute-start.2) | collective-permute-done | bytes 163872 | tf_op jit(solution)/shard_map/ppermute | solution.py:263
  76.2 0.1 rebuild.4
  76.3 17.8 %all_to_all.17.gathered = bf16[8,128,640]{2,1,0:T(8,128)(2,1)S(1)} all-to-all(bf16[8,128,640]{2,1,0:T(8,128)(2,1)S(1)} %rebuild.4), channel_id=1, replica_groups=mesh['section'=32,'tensor'=8,'dp'=2] {'tensor'}, dimensions={0} | all-to-all | bytes 2621440 | tf_op jit(solution)/shard_map/all_to_all | solution.py:257
  94.2 3.1 %tick.5 = (bf16[128,640]{1,0:T(8,128)(2,1)S(1)}, bf16[128,640]{1,0:T(8,128)(2,1)S(1)}, bf16[128,640]{1,0:T(8,128)(2,1)S(1)}) custom-call(s32[2,34]{1,0:T(2,128)S(1)} %bitcast.21, bf16[8,128,640]{2,1,0:T(8,128)(2,1)S(1)} %all_to_all.17.gathered, bf16[2560,640]{1,0:T(8,128)(2,1)S(1)} %bitcast.14, bf16[2560,640]{1,0:T(8,128)(2,1)S(1)} %collective-permute-done.w_other, ...), custom_call_target="tpu_custom_call" | custom-call | flops 838860800 | bytes 6553600 | tf_op jit(solution)/shard_map/tick/pallas_call | solution.py:181
  97.3 1.9 %collective-permute-start.3 = (bf16[128,640]{1,0:T(8,128)(2,1)S(1)}, bf16[128,640]{1,0:T(8,128)(2,1)S(1)}, u32[]{:S(2)}, u32[]{:S(2)}) collective-permute-start(bf16[128,640]{1,0:T(8,128)(2,1)S(1)} %get-tuple-element.19), channel_id=1, source_target_pairs={{0,16},{16,32},{32,48},{48,64},{64,80},{80,96},{96,112},{112,128},... | collective-permute-start | bytes 491528 | tf_op jit(solution)/shard_map/ppermute | solution.py:263
  99.2 0.8 maximum_bitcast_fusion
  100.1 8.1 %collective-permute-done.3.arriving = bf16[128,640]{1,0:T(8,128)(2,1)S(1)} collective-permute-done((bf16[128,640]{1,0:T(8,128)(2,1)S(1)}, bf16[128,640]{1,0:T(8,128)(2,1)S(1)}, u32[]{:S(2)}, u32[]{:S(2)}) %collective-permute-start.3) | collective-permute-done | bytes 163872 | tf_op jit(solution)/shard_map/ppermute | solution.py:263
  108.1 0.7 rebuild.5
  (1 shorter events, 0.0 us)
Async XLA Ops:
  0.6 27.2 %collective-permute-start = (bf16[2560,640]{1,0:T(8,128)(2,1)}, bf16[2560,640]{1,0:T(8,128)(2,1)S(1)}, u32[]{:S(2)}, u32[]{:S(2)}) collective-permute-start(bf16[2560,640]{1,0:T(8,128)(2,1)} %bitcast.11), channel_id=1, source_target_pairs={{0,1},{1,0},{2,3},{3,2},{4,5},{5,4},{6,7},{7,6},{8,9},{9,8},{10,11... | collective-permute-start | bytes 9830408 | tf_op jit(solution)/shard_map/ppermute | solution.py:251
  2.6 0.9 copy-start.1
  3.5 24.3 %copy-start = (bf16[1,2560,640]{2,1,0:T(8,128)(2,1)S(1)}, bf16[1,2560,640]{2,1,0:T(8,128)(2,1)}, u32[]{:S(2)}) copy-start(bf16[1,2560,640]{2,1,0:T(8,128)(2,1)} %param.14) | copy-start | bytes 9830404
  3.6 24.2 %copy-start.2 = (s32[34,2]{0,1:T(2,128)S(1)}, s32[34,2]{0,1:T(2,128)}, u32[]{:S(2)}) copy-start(s32[34,2]{0,1:T(2,128)} %param.16) | copy-start | bytes 820
  31.0 11.0 %collective-permute-start.1 = (bf16[128,640]{1,0:T(8,128)(2,1)S(1)}, bf16[128,640]{1,0:T(8,128)(2,1)S(1)}, u32[]{:S(2)}, u32[]{:S(2)}) collective-permute-start(bf16[128,640]{1,0:T(8,128)(2,1)S(1)} %get-tuple-element.13), channel_id=1, source_target_pairs={{0,16},{16,32},{32,48},{48,64},{64,80},{80,96},{96,112},{112,128},... | collective-permute-start | bytes 491528 | tf_op jit(solution)/shard_map/ppermute | solution.py:263
  65.3 10.9 %collective-permute-start.2 = (bf16[128,640]{1,0:T(8,128)(2,1)S(1)}, bf16[128,640]{1,0:T(8,128)(2,1)S(1)}, u32[]{:S(2)}, u32[]{:S(2)}) collective-permute-start(bf16[128,640]{1,0:T(8,128)(2,1)S(1)} %get-tuple-element.16), channel_id=1, source_target_pairs={{0,16},{16,32},{32,48},{48,64},{64,80},{80,96},{96,112},{112,128},... | collective-permute-start | bytes 491528 | tf_op jit(solution)/shard_map/ppermute | solution.py:263
  97.3 10.8 %collective-permute-start.3 = (bf16[128,640]{1,0:T(8,128)(2,1)S(1)}, bf16[128,640]{1,0:T(8,128)(2,1)S(1)}, u32[]{:S(2)}, u32[]{:S(2)}) collective-permute-start(bf16[128,640]{1,0:T(8,128)(2,1)S(1)} %get-tuple-element.19), channel_id=1, source_target_pairs={{0,16},{16,32},{32,48},{48,64},{64,80},{80,96},{96,112},{112,128},... | collective-permute-start | bytes 491528 | tf_op jit(solution)/shard_map/ppermute | solution.py:263
